TPU v7x, 256 devices: a whole 4x4x8 slice. The times are simulated.
256 devices in a mesh: seq: 32 (over y, z), chan: 8 (over x, core).
Axes of the slice: x: 4, y: 4, z: 8, core: 2. Of those that a mesh axis runs over, the one named last changes fastest.
Arguments:
- query_mr: bfloat16 [4096, 8192], P('seq', 'chan'), may hold values from -6 to 6
- key_mr: bfloat16 [4096, 8192], P('seq', 'chan'), may hold values from -6 to 6
- value_mr: bfloat16 [4096, 8192], P('seq', 'chan'), may hold values from -6 to 6
- query_li: bfloat16 [4096, 8192], P('seq', 'chan'), may hold values from -6 to 6
- key_li: bfloat16 [4096, 8192], P('seq', 'chan'), may hold values from -6 to 6
- cotangent: bfloat16 [4096, 8192], P('seq', 'chan'), may hold values from -40 to 40
- mr_filter: float32 [512, 128], P('chan'), may hold values from -3.535534 to 3.535534
- norm_gain: float32 [8192], P('chan'), may hold values from 0.1 to 1.9
- li_decay: float32 [512, 16], P('chan'), may hold values from 0.00012207031 to 0.03
- li_residue: float32 [512, 16], P('chan'), may hold values from -1 to 1
Outputs:
- out_li: bfloat16 [4096, 8192], P('seq', 'chan')
- grad_query_mr: bfloat16 [4096, 8192], P('seq', 'chan')
- grad_key_mr: bfloat16 [4096, 8192], P('seq', 'chan')
- grad_value_mr: bfloat16 [4096, 8192], P('seq', 'chan')
- grad_query_li: bfloat16 [4096, 8192], P('seq', 'chan')
- grad_key_li: bfloat16 [4096, 8192], P('seq', 'chan')
- grad_gain: float32 [8192], P('chan')
- grad_filter: float32 [512, 128], P('chan')
All inputs are finite; a program needn't handle non-finite values.
Results may differ from a plain program's by a relative error of at most 0.025.
Values may be sent and summed in bfloat16 or wider, within the bound.
A program may use at most 128 MiB of HBM per device.

v0:
```python
import jax
import jax.numpy as jnp
from jax import lax
from jax.sharding import PartitionSpec as P

D = 8192
G = 512
LBLK = 128
HIGHEST = lax.Precision.HIGHEST


def from_behind(value, axis, steps):
    count = lax.axis_size(axis)
    initial, last = (max(0, -steps), min(count, count - steps))
    return lax.ppermute(value, axis, [(source, source + steps) for source in range(initial, last)])


def toeplitz(edge_row):
    group_count, double_len = edge_row.shape
    block_len = double_len // 2
    cyclic = jnp.roll(jnp.flip(edge_row, -1), block_len + 1, axis=-1)
    repeated = jnp.tile(cyclic, (1, block_len))
    shaped = repeated[:, : block_len * (double_len - 1)].reshape(
        group_count, block_len, double_len - 1
    )
    return shaped[:, :, :block_len]


def combine_pair(earlier, latter):
    return (earlier[0] * latter[0], latter[1] + latter[0][..., None] * earlier[1])


def modal_parts(blocks, decays, residues, backward):
    block_len = blocks.shape[1]
    offsets = jnp.arange(block_len, dtype=jnp.float32)
    rate_col = decays[:, :, None]
    weights_res = residues * jnp.sqrt(2.0 * decays)
    fading = jnp.exp(-rate_col * offsets)
    filter_taps = jnp.einsum("gr,grd->gd", weights_res, fading, precision=HIGHEST)
    matrix = toeplitz(jnp.concatenate([jnp.zeros_like(filter_taps), filter_taps], -1))
    if backward:
        inside = jnp.einsum("gji,bjgc->bigc", matrix, blocks, precision=HIGHEST)
        weigh_in = fading
        weigh_out = weights_res[:, :, None] * jnp.exp(-rate_col * (block_len - offsets))
    else:
        inside = jnp.einsum("gij,bjgc->bigc", matrix, blocks, precision=HIGHEST)
        weigh_in = jnp.exp(-rate_col * (block_len - 1.0 - offsets))
        weigh_out = weights_res[:, :, None] * jnp.exp(-rate_col * (offsets + 1.0))
    states = jnp.einsum("grj,bjgc->bgrc", weigh_in, blocks, precision=HIGHEST)
    powers = jnp.broadcast_to(jnp.exp(-decays * block_len), (blocks.shape[0],) + decays.shape)
    running = lax.associative_scan(combine_pair, (powers, states), reverse=backward, axis=0)
    return (inside, weigh_out, running)


def modal_finish(inside, weigh_out, running, incoming, backward):
    powers, states = running
    if backward:
        prior_pow = jnp.concatenate([powers[1:], jnp.ones_like(powers[:1])], 0)
        prior_sum = jnp.concatenate([states[1:], jnp.zeros_like(states[:1])], 0)
    else:
        prior_pow = jnp.concatenate([jnp.ones_like(powers[:1]), powers[:-1]], 0)
        prior_sum = jnp.concatenate([jnp.zeros_like(states[:1]), states[:-1]], 0)
    entering = prior_sum + prior_pow[..., None] * incoming[None]
    return inside + jnp.einsum("gri,bgrc->bigc", weigh_out, entering, precision=HIGHEST)


def local_long(columns, decays, residues, backward):
    seq_len, chan_count = columns.shape
    group_size = D // G
    blocks = columns.reshape(seq_len // LBLK, LBLK, chan_count // group_size, group_size)
    inside, weigh_out, running = modal_parts(blocks, decays, residues, backward)
    incoming = jnp.zeros_like(running[1][0])
    return modal_finish(inside, weigh_out, running, incoming, backward).reshape(seq_len, chan_count)


def on_device(
    query_mr,
    key_mr,
    value_mr,
    query_li,
    key_li,
    cotangent,
    mr_filter,
    norm_gain,
    li_decay,
    li_residue,
):
    row_count, chan_count = query_mr.shape
    group_count, tap_count = mr_filter.shape
    group_size = chan_count // group_count
    block_count = row_count // tap_count
    grad_scale = float(row_count * lax.axis_size("seq")) ** (-0.5)
    taps_mr = mr_filter.astype(jnp.bfloat16)
    zero_taps = jnp.zeros_like(taps_mr)
    lower_band = toeplitz(jnp.concatenate([zero_taps, taps_mr], -1))
    upper_band = toeplitz(jnp.concatenate([taps_mr, zero_taps], -1))
    mixed_mr = (key_mr.astype(jnp.float32) * value_mr.astype(jnp.float32)).astype(jnp.bfloat16)
    rim_rows = from_behind(mixed_mr, "seq", 1)
    blocks = mixed_mr.reshape(block_count, tap_count, group_count, group_size)
    before = jnp.concatenate(
        [rim_rows.reshape(1, tap_count, group_count, group_size), blocks[:-1]], 0
    )
    conv_mr = jnp.einsum("gij,bjgc->bigc", lower_band, blocks, preferred_element_type=jnp.float32)
    conv_mr = conv_mr + jnp.einsum(
        "gij,bjgc->bigc", upper_band, before, preferred_element_type=jnp.float32
    )
    conv_mr = conv_mr.reshape(row_count, chan_count)
    out_mr = (query_mr.astype(jnp.float32) * conv_mr).astype(jnp.bfloat16)
    out_full = lax.optimization_barrier(out_mr).astype(jnp.float32)
    squares = lax.psum(jnp.sum(out_full * out_full, axis=1), "chan")
    inv_rms = lax.rsqrt(squares / D + 1e-06)[:, None]
    normed = out_full * inv_rms * norm_gain
    mixed_li = key_li.astype(jnp.float32) * normed
    cotan_full = cotangent.astype(jnp.float32)
    back_li = cotan_full * query_li.astype(jnp.float32)
    local_groups = group_count // lax.axis_size("seq")
    group_start = lax.axis_index("seq") * local_groups
    decays_here = lax.dynamic_slice_in_dim(li_decay, group_start, local_groups, 0)
    residues_here = lax.dynamic_slice_in_dim(li_residue, group_start, local_groups, 0)
    columns = lax.all_to_all(
        mixed_li.astype(jnp.bfloat16), "seq", split_axis=1, concat_axis=0, tiled=True
    ).astype(mixed_li.dtype)
    conv_li = lax.all_to_all(
        local_long(columns, decays_here, residues_here, False).astype(jnp.bfloat16),
        "seq",
        split_axis=0,
        concat_axis=1,
        tiled=True,
    ).astype(jnp.float32)
    grad_columns = lax.all_to_all(
        back_li.astype(jnp.bfloat16), "seq", split_axis=1, concat_axis=0, tiled=True
    ).astype(back_li.dtype)
    grad_mixed_li = lax.all_to_all(
        local_long(grad_columns, decays_here, residues_here, True),
        "seq",
        split_axis=0,
        concat_axis=1,
        tiled=True,
    )
    out_li = (query_li.astype(jnp.float32) * conv_li).astype(jnp.bfloat16)
    grad_query_li = (cotan_full * conv_li).astype(jnp.bfloat16)
    grad_key_li = (grad_mixed_li * normed).astype(jnp.bfloat16)
    grad_normed = grad_mixed_li * key_li.astype(jnp.float32)
    gain_part = jnp.sum(grad_normed * out_full * inv_rms, axis=0)
    weighted = grad_normed * norm_gain
    cross_dots = lax.psum(jnp.sum(weighted * out_full, axis=1), "chan")[:, None]
    grad_out_mr = inv_rms * weighted - out_full * inv_rms**3 * cross_dots / D
    grad_query_mr = (grad_out_mr * conv_mr).astype(jnp.bfloat16)
    back_mr = (grad_out_mr * query_mr.astype(jnp.float32)).astype(jnp.bfloat16)
    after_rim = from_behind(back_mr, "seq", -1)
    back_blocks = back_mr.reshape(block_count, tap_count, group_count, group_size)
    after_rows = jnp.concatenate(
        [back_blocks[1:], after_rim.reshape(1, tap_count, group_count, group_size)], 0
    )
    grad_mixed_mr = jnp.einsum(
        "gji,bjgc->bigc", lower_band, back_blocks, preferred_element_type=jnp.float32
    )
    grad_mixed_mr = grad_mixed_mr + jnp.einsum(
        "gji,bjgc->bigc", upper_band, after_rows, preferred_element_type=jnp.float32
    )
    grad_mixed_mr = grad_mixed_mr.reshape(row_count, chan_count)
    grad_key_mr = (grad_mixed_mr * value_mr.astype(jnp.float32)).astype(jnp.bfloat16)
    grad_value_mr = (grad_mixed_mr * key_mr.astype(jnp.float32)).astype(jnp.bfloat16)
    extended = jnp.concatenate([before, blocks], 1)
    gram_block = jnp.einsum(
        "bigc,bmgc->gim", back_blocks, extended, preferred_element_type=jnp.float32
    )
    flipped = jnp.flip(gram_block, -1)
    padded = jnp.pad(flipped, ((0, 0), (0, 0), (0, 1)))
    flattened = padded.reshape(group_count, -1)
    skewed = flattened[:, tap_count - 1 : tap_count - 1 + 2 * tap_count * tap_count]
    skewed = skewed.reshape(group_count, tap_count, 2 * tap_count)[:, :, :tap_count]
    filter_part = jnp.sum(skewed, axis=1)
    param_sums = (
        lax.psum(gain_part.astype(jnp.bfloat16), "seq").astype(jnp.float32),
        lax.psum(filter_part.astype(jnp.bfloat16), "seq").astype(jnp.float32),
    )
    grad_gain = param_sums[0] * grad_scale
    grad_filter = param_sums[1] * grad_scale
    return (
        out_li,
        grad_query_mr,
        grad_key_mr,
        grad_value_mr,
        grad_query_li,
        grad_key_li,
        grad_gain,
        grad_filter,
    )


def solution(mesh):
    in_specs = (
        P("seq", "chan"),
        P("seq", "chan"),
        P("seq", "chan"),
        P("seq", "chan"),
        P("seq", "chan"),
        P("seq", "chan"),
        P("chan", None),
        P("chan"),
        P("chan", None),
        P("chan", None),
    )
    out_specs = (
        P("seq", "chan"),
        P("seq", "chan"),
        P("seq", "chan"),
        P("seq", "chan"),
        P("seq", "chan"),
        P("seq", "chan"),
        P("chan"),
        P("chan", None),
    )
    return jax.shard_map(
        on_device, mesh=mesh, in_specs=in_specs, out_specs=out_specs, check_vma=False
    )
```

profile of v0, /device:TPU:32, one launch (start us, length us, event | category | flops | bytes accessed | tf_op | source)
XLA Modules:
  0.0 443.5 jit_solution(472008142492113452)
XLA Ops:
  0.7 1.1 copy.227
  1.8 1.1 copy.245
  2.9 0.8 fusion.24
  3.7 11.5 %all-to-all-start.2 = ((bf16[128,32,32]{0,2,1:T(8,128)(2,1)}), bf16[128,32,32]{0,2,1:T(8,128)(2,1)S(1)}, u32[]{:S(2)}, u32[]{:S(2)}) async-start(bf16[128,32,32]{0,2,1:T(8,128)(2,1)} %bitcast.30), calls=%async_computation.2 | async-start | bytes 524288 | tf_op jit(solution)/shard_map/all_to_all | solution.py:130
  15.2 1.1 copy.230
  16.3 1.1 copy.231
  17.6 3.4 collective-permute-start
  26.5 0.7 slice_multiply_fusion
  34.2 2.6 copy.273
  36.8 2.2 slice.458
  39.0 15.9 %reshape.167 = bf16[64,128,255]{2,1,0:T(8,128)(2,1)} reshape(bf16[64,32640]{1,0:T(8,128)(2,1)} %slice.458) | data formatting | bytes 8355840 | tf_op jit(solution)/shard_map/reshape | solution.py:23
  55.2 2.6 copy.274
  57.8 2.2 slice.460
  60.0 15.9 %reshape.169 = bf16[64,128,255]{2,1,0:T(8,128)(2,1)} reshape(bf16[64,32640]{1,0:T(8,128)(2,1)} %slice.460) | data formatting | bytes 8355840 | tf_op jit(solution)/shard_map/reshape | solution.py:23
  77.0 3.6 fusion.6
  85.5 0.7 add.314
  86.6 11.2 %pad.305 = f32[32,2,16,16]{2,3,0,1:T(8,128)S(1)} pad(f32[16,2,16,16]{2,3,0,1:T(8,128)} %add.314, f32[]{:T(128)} %constant.15.clone.1), padding=1_0_1x0_0_0x0_0_0x0_0_0 | pad | bytes 98308
  97.8 0.9 slice_add_fusion.2
  98.7 1.9 slice.444
  100.9 1.7 fusion.14
  102.6 0.9 copy.257
  103.5 8.9 %all-to-all-start.3 = ((f32[32,128,32]{1,2,0:T(8,128)}), f32[32,128,32]{1,2,0:T(8,128)S(1)}, u32[]{:S(2)}, u32[]{:S(2)}) async-start(f32[32,128,32]{1,2,0:T(8,128)} %bitcast.140), calls=%async_computation.3 | async-start | bytes 1048576 | tf_op jit(solution)/shard_map/all_to_all | solution.py:133
  112.4 2.9 fusion.8
  115.6 13.8 %psum.28 = f32[128]{0:T(128)S(1)} all-reduce(f32[128]{0:T(128)S(1)} %fusion.26), channel_id=1, replica_groups=mesh['seq'=32,'chan'=8] {'chan'}, use_global_device_ids=true, to_apply=%region_1.2 | all-reduce | flops 128 | bytes 1024 | tf_op jit(solution)/shard_map/psum | solution.py:110
  129.8 12.4 %psum.29 = f32[128]{0:T(128)S(1)} all-reduce(f32[128]{0:T(128)S(1)} %get-tuple-element.49), channel_id=1, replica_groups=mesh['seq'=32,'chan'=8] {'chan'}, use_global_device_ids=true, to_apply=%region_3.4 | all-reduce | flops 128 | bytes 1024 | tf_op jit(solution)/shard_map/psum | solution.py:146
  142.2 1.3 fusion.20
  143.4 1.8 copy.259
  145.2 9.5 %all-to-all-start = ((bf16[128,32,32]{0,2,1:T(8,128)(2,1)}), bf16[128,32,32]{0,2,1:T(8,128)(2,1)S(1)}, u32[]{:S(2)}, u32[]{:S(2)}) async-start(bf16[128,32,32]{0,2,1:T(8,128)(2,1)} %bitcast.141), calls=%async_computation | async-start | bytes 524288 | tf_op jit(solution)/shard_map/all_to_all | solution.py:120
  154.8 1.8 copy.263
  156.5 2.1 collective-permute-start.1
  158.7 5.5 %fusion.36 = f32[64,128,256]{2,1,0:T(8,128)} fusion(bf16[128,64,16]{0,2,1:T(8,128)(2,1)S(1)} %bitcast.138, bf16[1,128,64,16]{1,3,2,0:T(8,128)(2,1)S(1)} %bitcast.137, bf16[1,128,64,16]{1,3,2,0:T(8,128)(2,1)} %bitcast.55), kind=kOutput, calls=%fused_computation.53 | convolution fusion | flops 68157440 | bytes 9175040 | tf_op jit(solution)/shard_map/bigc,bmgc->gim/dot_general | solution.py:165
  164.2 67.4 %rev.14 = f32[64,128,256]{2,1,0:T(8,128)} reverse(f32[64,128,256]{2,1,0:T(8,128)} %fusion.36), dimensions={2} | reverse | bytes 16777216 | tf_op jit(solution)/shard_map/jit(_flip)/rev | solution.py:168
  231.5 9.6 %pad.177 = f32[64,128,257]{2,1,0:T(8,128)} pad(f32[64,128,256]{2,1,0:T(8,128)} %rev.14, f32[]{:T(128)} %constant.15.clone.1), padding=0_0x0_0x0_1 | pad | bytes 16809988 | tf_op jit(solution)/shard_map/jit(_pad)/pad | solution.py:169
  241.1 12.2 %reshape.180 = f32[64,32896]{1,0:T(8,128)} reshape(f32[64,128,257]{2,1,0:T(8,128)} %pad.177) | data formatting | bytes 16842752 | tf_op jit(solution)/shard_map/reshape | solution.py:170
  253.3 5.6 %slice.516 = f32[64,32768]{1,0:T(8,128)S(1)} slice(f32[64,32896]{1,0:T(8,128)} %reshape.180), slice={[0:64], [127:32895]} | slice | bytes 16777216 | tf_op jit(solution)/shard_map/slice | solution.py:171
  258.9 2.5 copy.276
  262.0 139.5 %all-reduce.49 = (bf16[1024]{0:T(1024)(128)(2,1)S(1)}, bf16[64,128]{1,0:T(8,128)(2,1)S(1)}) all-reduce(bf16[1024]{0:T(1024)(128)(2,1)S(1)} %get-tuple-element.48, bf16[64,128]{1,0:T(8,128)(2,1)S(1)} %slice_reduce_fusion), channel_id=1, replica_groups=mesh['seq'=32,'chan'=8] {'seq'}, use_global_device_ids=true, to_apply=%region_5.6 | all-reduce | flops 9216 | bytes 36864 | tf_op jit(solution)/shard_map/psum | solution.py:175
  402.7 2.2 fusion.4
  406.5 0.7 add.291
  407.5 11.2 %pad.303 = f32[32,2,16,16]{2,3,0,1:T(8,128)S(1)} pad(f32[16,2,16,16]{2,3,0,1:T(8,128)} %add.291, f32[]{:T(128)} %constant.15.clone.1), padding=1_0_1x0_0_0x0_0_0x0_0_0 | pad | bytes 98308
  418.8 1.3 fusion.52
  421.5 9.1 %all-to-all-start.1 = ((bf16[32,128,32]{1,2,0:T(8,128)(2,1)}), bf16[32,128,32]{1,2,0:T(8,128)(2,1)S(1)}, u32[]{:S(2)}, u32[]{:S(2)}) async-start(bf16[32,128,32]{1,2,0:T(8,128)(2,1)} %bitcast.27), calls=%async_computation.1 | async-start | bytes 524288 | tf_op jit(solution)/shard_map/all_to_all | solution.py:123
  430.6 2.3 fusion.11
  433.1 0.9 copy.261
  433.9 0.8 copy.260
  434.8 6.9 %all-to-all-done.1 = bf16[32,128,32]{1,2,0:T(8,128)(2,1)S(1)} async-done(((bf16[32,128,32]{1,2,0:T(8,128)(2,1)}), bf16[32,128,32]{1,2,0:T(8,128)(2,1)S(1)}, u32[]{:S(2)}, u32[]{:S(2)}) %all-to-all-start.1) | async-done | bytes 262176 | tf_op jit(solution)/shard_map/all_to_all | solution.py:123
  441.8 0.9 copy.262
  442.7 0.8 copy.258
  (210 shorter events, 24.8 us)
Async XLA Ops:
  0.6 20.3 %copy-start.10 = (f32[64,16]{0,1:T(8,128)S(1)}, f32[64,16]{0,1:T(8,128)}, u32[]{:S(2)}) copy-start(f32[64,16]{0,1:T(8,128)} %param.19) | copy-start | bytes 12292
  0.6 20.3 %copy-start.9 = (f32[64,16]{0,1:T(8,128)S(1)}, f32[64,16]{0,1:T(8,128)}, u32[]{:S(2)}) copy-start(f32[64,16]{0,1:T(8,128)} %param.18) | copy-start | bytes 12292
  0.7 29.6 %copy-start.3 = (f32[64,128]{1,0:T(8,128)S(1)}, f32[64,128]{1,0:T(8,128)}, u32[]{:S(2)}) copy-start(f32[64,128]{1,0:T(8,128)} %param.16) | copy-start | bytes 98308
  2.9 30.5 %copy-start.1 = (bf16[128,1024]{1,0:T(8,128)(2,1)S(1)}, bf16[128,1024]{1,0:T(8,128)(2,1)}, u32[]{:S(2)}) copy-start(bf16[128,1024]{1,0:T(8,128)(2,1)} %param.10) | copy-start | bytes 786436
  3.7 29.9 %copy-start.2 = (bf16[128,1024]{1,0:T(8,128)(2,1)S(1)}, bf16[128,1024]{1,0:T(8,128)(2,1)}, u32[]{:S(2)}) copy-start(bf16[128,1024]{1,0:T(8,128)(2,1)} %param.14) | copy-start | bytes 786436
  3.7 76.9 %all-to-all-start.2 = ((bf16[128,32,32]{0,2,1:T(8,128)(2,1)}), bf16[128,32,32]{0,2,1:T(8,128)(2,1)S(1)}, u32[]{:S(2)}, u32[]{:S(2)}) async-start(bf16[128,32,32]{0,2,1:T(8,128)(2,1)} %bitcast.30), calls=%async_computation.2 | async-start | bytes 524288 | tf_op jit(solution)/shard_map/all_to_all | solution.py:130
  17.6 94.9 %collective-permute-start = (bf16[128,1024]{0,1:T(8,128)(2,1)S(1)}, bf16[128,1024]{0,1:T(8,128)(2,1)}, u32[]{:S(2)}, u32[]{:S(2)}) collective-permute-start(bf16[128,1024]{0,1:T(8,128)(2,1)S(1)} %fusion.22), channel_id=1, source_target_pairs={{0,8},{8,16},{16,24},{24,32},{32,40},{40,48},{48,56},{56,64},{64,7... | collective-permute-start | bytes 786440 | tf_op jit(solution)/shard_map/ppermute | solution.py:15
  21.8 7.3 %copy-start.6 = (f32[2,16]{1,0:T(2,128)}, f32[2,16]{1,0:T(2,128)S(1)}, u32[]{:S(2)}) copy-start(f32[2,16]{1,0:T(2,128)S(1)} %get-tuple-element.92) | copy-start | bytes 388
  33.4 67.1 %copy-start = (f32[2,128,255]{2,1,0:T(8,128)}, f32[2,128,255]{2,1,0:T(8,128)S(1)}, u32[]{:S(2)}) copy-start(f32[2,128,255]{2,1,0:T(8,128)S(1)} %reshape.172) | copy-start | bytes 783364
  85.1 15.8 %copy-start.7 = (f32[2,16]{1,0:T(2,128)S(1)}, f32[2,16]{1,0:T(2,128)}, u32[]{:S(2)}) copy-start(f32[2,16]{1,0:T(2,128)} %copy-done.6) | copy-start | bytes 388
  85.1 15.8 %copy-start.12 = (f32[128]{0:T(128)S(1)}, f32[128]{0:T(128)}, u32[]{:S(2)}) copy-start(f32[128]{0:T(128)} %iota_subtract_fusion) | copy-start | bytes 1540
  100.9 28.4 %copy-start.4 = (f32[1024]{0:T(1024)S(1)}, f32[1024]{0:T(1024)}, u32[]{:S(2)}) copy-start(f32[1024]{0:T(1024)} %param.17) | copy-start | bytes 12292
  103.5 25.9 %all-to-all-start.3 = ((f32[32,128,32]{1,2,0:T(8,128)}), f32[32,128,32]{1,2,0:T(8,128)S(1)}, u32[]{:S(2)}, u32[]{:S(2)}) async-start(f32[32,128,32]{1,2,0:T(8,128)} %bitcast.140), calls=%async_computation.3 | async-start | bytes 1048576 | tf_op jit(solution)/shard_map/all_to_all | solution.py:133
  145.2 259.7 %all-to-all-start = ((bf16[128,32,32]{0,2,1:T(8,128)(2,1)}), bf16[128,32,32]{0,2,1:T(8,128)(2,1)S(1)}, u32[]{:S(2)}, u32[]{:S(2)}) async-start(bf16[128,32,32]{0,2,1:T(8,128)(2,1)} %bitcast.141), calls=%async_computation | async-start | bytes 524288 | tf_op jit(solution)/shard_map/all_to_all | solution.py:120
  156.5 274.1 %collective-permute-start.1 = (bf16[128,1024]{0,1:T(8,128)(2,1)S(1)}, bf16[128,1024]{0,1:T(8,128)(2,1)}, u32[]{:S(2)}, u32[]{:S(2)}) collective-permute-start(bf16[128,1024]{0,1:T(8,128)(2,1)S(1)} %get-tuple-element.52), channel_id=1, source_target_pairs={{8,0},{16,8},{24,16},{32,24},{40,32},{48,40},{56,48},{64,56},{72,6... | collective-permute-start | bytes 786440 | tf_op jit(solution)/shard_map/ppermute | solution.py:15
  261.4 143.5 %copy-start.13 = (f32[128]{0:T(128)S(1)}, f32[128]{0:T(128)}, u32[]{:S(2)}) copy-start(f32[128]{0:T(128)} %iota_subtract_fusion.1) | copy-start | bytes 1540
  261.5 144.1 %copy-start.5 = (f32[2,16]{1,0:T(2,128)S(1)}, f32[2,16]{1,0:T(2,128)}, u32[]{:S(2)}) copy-start(f32[2,16]{1,0:T(2,128)} %get-tuple-element.82) | copy-start | bytes 388
  261.5 144.1 %copy-start.11 = (f32[2,16]{1,0:T(2,128)S(1)}, f32[2,16]{1,0:T(2,128)}, u32[]{:S(2)}) copy-start(f32[2,16]{1,0:T(2,128)} %get-tuple-element.89) | copy-start | bytes 388
  405.9 14.3 %copy-start.8 = (f32[2,16]{1,0:T(2,128)S(1)}, f32[2,16]{1,0:T(2,128)}, u32[]{:S(2)}) copy-start(f32[2,16]{1,0:T(2,128)} %copy-done.6) | copy-start | bytes 388
  421.5 20.2 %all-to-all-start.1 = ((bf16[32,128,32]{1,2,0:T(8,128)(2,1)}), bf16[32,128,32]{1,2,0:T(8,128)(2,1)S(1)}, u32[]{:S(2)}, u32[]{:S(2)}) async-start(bf16[32,128,32]{1,2,0:T(8,128)(2,1)} %bitcast.27), calls=%async_computation.1 | async-start | bytes 524288 | tf_op jit(solution)/shard_map/all_to_all | solution.py:123
where the time goes:
time: 451 us; the launch traced here: 444 us
  local copies, waits for them, and re-layouts  188 us (42%)
  blocking collectives  166 us (37%)
  starting transfers between devices  44.5 us (10%)
  matrix products  21.6 us (5%)
  other arithmetic  15.6 us (3%)
  waiting for transfers between devices  6.91 us (2%)
    psum x1, blocking collectives, on_device(): lax.psum(gain_part.astype(jnp.bfloat16), 'seq').astype(jnp.float32)  139 us
    rev x1, local copies, waits for them, and re-layouts, on_device(): flipped = jnp.flip(gram_block, -1)  67.4 us
    unnamed x57, local copies, waits for them, and re-layouts  43.6 us
    reshape x3, local copies, waits for them, and re-layouts, toeplitz(): repeated[:, :block_len * (double_len - 1)]  32.2 us
    psum x1, blocking collectives, on_device(): squares = lax.psum(jnp.sum(out_full * out_full, axis=1), 'chan')  13.8 us
    psum x1, blocking collectives, on_device(): cross_dots = lax.psum(jnp.sum(weighted * out_full, axis=1), 'chan')[:, None]  12.4 us
    reshape x1, local copies, waits for them, and re-layouts, on_device(): flattened = padded.reshape(group_count, -1)  12.2 us
    all_to_all x1, starting transfers between devices, on_device(): lax.all_to_all(back_li.astype(jnp.bfloat16), 'seq', split_axis=1, concat_...  11.5 us
  transfers between devices with their start and end apart: 6, of which 1 were waited for; matrix products, arithmetic and copies ran while one was open for 49% of the time, Pallas kernels for 0%

commit v1 on v0

--- a/solution.py
+++ b/solution.py
@@ -172,7 +172,7 @@
     skewed = skewed.reshape(group_count, tap_count, 2 * tap_count)[:, :, :tap_count]
     filter_part = jnp.sum(skewed, axis=1)
     param_sums = (
-        lax.psum(gain_part.astype(jnp.bfloat16), "seq").astype(jnp.float32),
+        jnp.sum(lax.all_gather(gain_part.astype(jnp.bfloat16), "seq"), axis=0).astype(jnp.float32),
         lax.psum(filter_part.astype(jnp.bfloat16), "seq").astype(jnp.float32),
     )
     grad_gain = param_sums[0] * grad_scale

time: 451 us -> 499 us (1.11)
  blocking collectives: 166 us -> 214 us
    all_gather x0 -> x1, blocking collectives: none -> 50.1 us  [on_device(): lax.all_gather(gain_part.astype(jnp.bfloat16), 'seq')]
    unnamed x57 -> x55, local copies, waits for them, and re-layouts: 43.6 us -> 43.6 us
  transfers between devices with their start and end apart: 6 -> 6, of which waited for: 1 -> 1; matrix products, arithmetic and copies ran while one was open for 49% -> 44% of each run, Pallas kernels for 0% -> 0%
where the time goes in v1:
time: 499 us; the launch traced here: 492 us
  blocking collectives  214 us (43%)
  local copies, waits for them, and re-layouts  188 us (38%)
  starting transfers between devices  44.3 us (9%)
  matrix products  21.6 us (4%)
  other arithmetic  15.6 us (3%)
  waiting for transfers between devices  6.91 us (1%)
    psum x1, blocking collectives, on_device(): lax.psum(filter_part.astype(jnp.bfloat16), 'seq').astype(jnp.float32)  138 us
    rev x1, local copies, waits for them, and re-layouts, on_device(): flipped = jnp.flip(gram_block, -1)  67.4 us
    all_gather x1, blocking collectives, on_device(): lax.all_gather(gain_part.astype(jnp.bfloat16), 'seq')  50.1 us
    unnamed x55, local copies, waits for them, and re-layouts  43.6 us
    reshape x3, local copies, waits for them, and re-layouts, toeplitz(): repeated[:, :block_len * (double_len - 1)]  32.1 us
    psum x1, blocking collectives, on_device(): squares = lax.psum(jnp.sum(out_full * out_full, axis=1), 'chan')  13.8 us
    psum x1, blocking collectives, on_device(): cross_dots = lax.psum(jnp.sum(weighted * out_full, axis=1), 'chan')[:, None]  12.4 us
    reshape x1, local copies, waits for them, and re-layouts, on_device(): flattened = padded.reshape(group_count, -1)  12.2 us
  transfers between devices with their start and end apart: 6, of which 1 were waited for; matrix products, arithmetic and copies ran while one was open for 44% of the time, Pallas kernels for 0%

profile of v1, /device:TPU:32, one launch (start us, length us, event | category | flops | bytes accessed | tf_op | source)
XLA Modules:
  0.0 492.0 jit_solution(6958982823771989033)
XLA Ops:
  0.7 1.1 copy.323
  1.8 1.1 copy.341
  2.9 0.8 fusion.24
  3.7 11.5 %all-to-all-start.2 = ((bf16[128,32,32]{0,2,1:T(8,128)(2,1)}), bf16[128,32,32]{0,2,1:T(8,128)(2,1)S(1)}, u32[]{:S(2)}, u32[]{:S(2)}) async-start(bf16[128,32,32]{0,2,1:T(8,128)(2,1)} %bitcast.30), calls=%async_computation.2 | async-start | bytes 524288 | tf_op jit(solution)/shard_map/all_to_all | solution.py:130
  15.2 1.1 copy.326
  16.3 1.1 copy.327
  17.6 3.4 collective-permute-start
  34.2 2.6 copy.369
  36.8 2.2 slice.458
  39.0 15.9 %reshape.175 = bf16[64,128,255]{2,1,0:T(8,128)(2,1)} reshape(bf16[64,32640]{1,0:T(8,128)(2,1)} %slice.458) | data formatting | bytes 8355840 | tf_op jit(solution)/shard_map/reshape | solution.py:23
  55.2 2.6 copy.370
  57.8 2.2 slice.460
  60.0 15.8 %reshape.177 = bf16[64,128,255]{2,1,0:T(8,128)(2,1)} reshape(bf16[64,32640]{1,0:T(8,128)(2,1)} %slice.460) | data formatting | bytes 8355840 | tf_op jit(solution)/shard_map/reshape | solution.py:23
  76.9 3.6 fusion.6
  85.4 0.7 add.312
  86.6 11.2 %pad.305 = f32[32,2,16,16]{2,3,0,1:T(8,128)S(1)} pad(f32[16,2,16,16]{2,3,0,1:T(8,128)} %add.312, f32[]{:T(128)} %constant.15.clone.1), padding=1_0_1x0_0_0x0_0_0x0_0_0 | pad | bytes 98308
  97.8 0.9 slice_add_fusion.2
  98.6 1.8 slice.444
  100.9 1.7 fusion.14
  102.6 0.9 copy.353
  103.4 8.9 %all-to-all-start.3 = ((f32[32,128,32]{1,2,0:T(8,128)}), f32[32,128,32]{1,2,0:T(8,128)S(1)}, u32[]{:S(2)}, u32[]{:S(2)}) async-start(f32[32,128,32]{1,2,0:T(8,128)} %bitcast.140), calls=%async_computation.3 | async-start | bytes 1048576 | tf_op jit(solution)/shard_map/all_to_all | solution.py:133
  112.4 2.9 fusion.8
  115.5 13.8 %psum.21 = f32[128]{0:T(128)S(1)} all-reduce(f32[128]{0:T(128)S(1)} %fusion.26), channel_id=1, replica_groups=mesh['seq'=32,'chan'=8] {'chan'}, use_global_device_ids=true, to_apply=%region_1.2 | all-reduce | flops 128 | bytes 1024 | tf_op jit(solution)/shard_map/psum | solution.py:110
  129.7 12.4 %psum.22 = f32[128]{0:T(128)S(1)} all-reduce(f32[128]{0:T(128)S(1)} %get-tuple-element.65), channel_id=1, replica_groups=mesh['seq'=32,'chan'=8] {'chan'}, use_global_device_ids=true, to_apply=%region_3.4 | all-reduce | flops 128 | bytes 1024 | tf_op jit(solution)/shard_map/psum | solution.py:146
  142.1 1.3 fusion.20
  143.4 1.8 copy.355
  145.2 9.5 %all-to-all-start = ((bf16[128,32,32]{0,2,1:T(8,128)(2,1)}), bf16[128,32,32]{0,2,1:T(8,128)(2,1)S(1)}, u32[]{:S(2)}, u32[]{:S(2)}) async-start(bf16[128,32,32]{0,2,1:T(8,128)(2,1)} %bitcast.141), calls=%async_computation | async-start | bytes 524288 | tf_op jit(solution)/shard_map/all_to_all | solution.py:120
  154.7 50.1 %all-gather = bf16[32768]{0:T(1024)(128)(2,1)S(1)} all-gather(bf16[1024]{0:T(1024)(128)(2,1)S(1)} %get-tuple-element.64), channel_id=2, replica_groups=mesh['seq'=32,'chan'=8] {'seq'}, dimensions={0}, use_global_device_ids=true | all-gather | bytes 67584 | tf_op jit(solution)/shard_map/all_gather | solution.py:175
  204.9 1.8 copy.359
  206.7 1.9 collective-permute-start.1
  208.6 5.5 %fusion.36 = f32[64,128,256]{2,1,0:T(8,128)} fusion(bf16[128,64,16]{0,2,1:T(8,128)(2,1)S(1)} %bitcast.138, bf16[1,128,64,16]{1,3,2,0:T(8,128)(2,1)S(1)} %bitcast.137, bf16[1,128,64,16]{1,3,2,0:T(8,128)(2,1)} %bitcast.55), kind=kOutput, calls=%fused_computation.53 | convolution fusion | flops 68157440 | bytes 9175040 | tf_op jit(solution)/shard_map/bigc,bmgc->gim/dot_general | solution.py:165
  214.1 67.4 %rev.14 = f32[64,128,256]{2,1,0:T(8,128)} reverse(f32[64,128,256]{2,1,0:T(8,128)} %fusion.36), dimensions={2} | reverse | bytes 16777216 | tf_op jit(solution)/shard_map/jit(_flip)/rev | solution.py:168
  281.5 9.5 %pad.177 = f32[64,128,257]{2,1,0:T(8,128)} pad(f32[64,128,256]{2,1,0:T(8,128)} %rev.14, f32[]{:T(128)} %constant.15.clone.1), padding=0_0x0_0x0_1 | pad | bytes 16809988 | tf_op jit(solution)/shard_map/jit(_pad)/pad | solution.py:169
  291.0 12.2 %reshape.188 = f32[64,32896]{1,0:T(8,128)} reshape(f32[64,128,257]{2,1,0:T(8,128)} %pad.177) | data formatting | bytes 16842752 | tf_op jit(solution)/shard_map/reshape | solution.py:170
  303.2 5.6 %slice.516 = f32[64,32768]{1,0:T(8,128)S(1)} slice(f32[64,32896]{1,0:T(8,128)} %reshape.188), slice={[0:64], [127:32895]} | slice | bytes 16777216 | tf_op jit(solution)/shard_map/slice | solution.py:171
  308.8 2.5 copy.372
  311.9 138.1 %psum.23 = bf16[64,128]{1,0:T(8,128)(2,1)S(1)} all-reduce(bf16[64,128]{1,0:T(8,128)(2,1)S(1)} %slice_reduce_fusion), channel_id=1, replica_groups=mesh['seq'=32,'chan'=8] {'seq'}, use_global_device_ids=true, to_apply=%region_7.8 | all-reduce | flops 8192 | bytes 32768 | tf_op jit(solution)/shard_map/psum | solution.py:176
  451.2 2.2 fusion.4
  455.0 0.7 add.289
  456.1 11.2 %pad.303 = f32[32,2,16,16]{2,3,0,1:T(8,128)S(1)} pad(f32[16,2,16,16]{2,3,0,1:T(8,128)} %add.289, f32[]{:T(128)} %constant.15.clone.1), padding=1_0_1x0_0_0x0_0_0x0_0_0 | pad | bytes 98308
  467.3 1.3 fusion.52
  470.0 9.1 %all-to-all-start.1 = ((bf16[32,128,32]{1,2,0:T(8,128)(2,1)}), bf16[32,128,32]{1,2,0:T(8,128)(2,1)S(1)}, u32[]{:S(2)}, u32[]{:S(2)}) async-start(bf16[32,128,32]{1,2,0:T(8,128)(2,1)} %bitcast.27), calls=%async_computation.1 | async-start | bytes 524288 | tf_op jit(solution)/shard_map/all_to_all | solution.py:123
  479.1 2.3 fusion.11
  481.6 0.9 copy.357
  482.4 0.8 copy.356
  483.3 6.9 %all-to-all-done.1 = bf16[32,128,32]{1,2,0:T(8,128)(2,1)S(1)} async-done(((bf16[32,128,32]{1,2,0:T(8,128)(2,1)}), bf16[32,128,32]{1,2,0:T(8,128)(2,1)S(1)}, u32[]{:S(2)}, u32[]{:S(2)}) %all-to-all-start.1) | async-done | bytes 262176 | tf_op jit(solution)/shard_map/all_to_all | solution.py:123
  490.3 0.9 copy.358
  491.2 0.8 copy.354
  (211 shorter events, 25.6 us)
Async XLA Ops:
  0.6 20.3 %copy-start.9 = (f32[64,16]{0,1:T(8,128)S(1)}, f32[64,16]{0,1:T(8,128)}, u32[]{:S(2)}) copy-start(f32[64,16]{0,1:T(8,128)} %param.19) | copy-start | bytes 12292
  0.6 20.3 %copy-start.8 = (f32[64,16]{0,1:T(8,128)S(1)}, f32[64,16]{0,1:T(8,128)}, u32[]{:S(2)}) copy-start(f32[64,16]{0,1:T(8,128)} %param.18) | copy-start | bytes 12292
  0.7 29.6 %copy-start.3 = (f32[64,128]{1,0:T(8,128)S(1)}, f32[64,128]{1,0:T(8,128)}, u32[]{:S(2)}) copy-start(f32[64,128]{1,0:T(8,128)} %param.16) | copy-start | bytes 98308
  2.9 30.5 %copy-start.1 = (bf16[128,1024]{1,0:T(8,128)(2,1)S(1)}, bf16[128,1024]{1,0:T(8,128)(2,1)}, u32[]{:S(2)}) copy-start(bf16[128,1024]{1,0:T(8,128)(2,1)} %param.10) | copy-start | bytes 786436
  3.7 29.9 %copy-start.2 = (bf16[128,1024]{1,0:T(8,128)(2,1)S(1)}, bf16[128,1024]{1,0:T(8,128)(2,1)}, u32[]{:S(2)}) copy-start(bf16[128,1024]{1,0:T(8,128)(2,1)} %param.14) | copy-start | bytes 786436
  3.7 76.8 %all-to-all-start.2 = ((bf16[128,32,32]{0,2,1:T(8,128)(2,1)}), bf16[128,32,32]{0,2,1:T(8,128)(2,1)S(1)}, u32[]{:S(2)}, u32[]{:S(2)}) async-start(bf16[128,32,32]{0,2,1:T(8,128)(2,1)} %bitcast.30), calls=%async_computation.2 | async-start | bytes 524288 | tf_op jit(solution)/shard_map/all_to_all | solution.py:130
  17.6 94.8 %collective-permute-start = (bf16[128,1024]{0,1:T(8,128)(2,1)S(1)}, bf16[128,1024]{0,1:T(8,128)(2,1)}, u32[]{:S(2)}, u32[]{:S(2)}) collective-permute-start(bf16[128,1024]{0,1:T(8,128)(2,1)S(1)} %fusion.22), channel_id=1, source_target_pairs={{0,8},{8,16},{16,24},{24,32},{32,40},{40,48},{48,56},{56,64},{64,7... | collective-permute-start | bytes 786440 | tf_op jit(solution)/shard_map/ppermute | solution.py:15
  21.8 7.3 %copy-start.6 = (f32[2,16]{1,0:T(2,128)}, f32[2,16]{1,0:T(2,128)S(1)}, u32[]{:S(2)}) copy-start(f32[2,16]{1,0:T(2,128)S(1)} %get-tuple-element.106) | copy-start | bytes 388
  33.5 67.0 %copy-start = (f32[2,128,255]{2,1,0:T(8,128)}, f32[2,128,255]{2,1,0:T(8,128)S(1)}, u32[]{:S(2)}) copy-start(f32[2,128,255]{2,1,0:T(8,128)S(1)} %reshape.180) | copy-start | bytes 783364
  85.0 15.8 %copy-start.7 = (f32[2,16]{1,0:T(2,128)S(1)}, f32[2,16]{1,0:T(2,128)}, u32[]{:S(2)}) copy-start(f32[2,16]{1,0:T(2,128)} %copy-done.6) | copy-start | bytes 388
  85.0 15.8 %copy-start.11 = (f32[128]{0:T(128)S(1)}, f32[128]{0:T(128)}, u32[]{:S(2)}) copy-start(f32[128]{0:T(128)} %iota_subtract_fusion) | copy-start | bytes 1540
  100.9 28.4 %copy-start.4 = (f32[1024]{0:T(1024)S(1)}, f32[1024]{0:T(1024)}, u32[]{:S(2)}) copy-start(f32[1024]{0:T(1024)} %param.17) | copy-start | bytes 12292
  103.4 25.9 %all-to-all-start.3 = ((f32[32,128,32]{1,2,0:T(8,128)}), f32[32,128,32]{1,2,0:T(8,128)S(1)}, u32[]{:S(2)}, u32[]{:S(2)}) async-start(f32[32,128,32]{1,2,0:T(8,128)} %bitcast.140), calls=%async_computation.3 | async-start | bytes 1048576 | tf_op jit(solution)/shard_map/all_to_all | solution.py:133
  145.2 308.3 %all-to-all-start = ((bf16[128,32,32]{0,2,1:T(8,128)(2,1)}), bf16[128,32,32]{0,2,1:T(8,128)(2,1)S(1)}, u32[]{:S(2)}, u32[]{:S(2)}) async-start(bf16[128,32,32]{0,2,1:T(8,128)(2,1)} %bitcast.141), calls=%async_computation | async-start | bytes 524288 | tf_op jit(solution)/shard_map/all_to_all | solution.py:120
  206.7 272.4 %collective-permute-start.1 = (bf16[128,1024]{0,1:T(8,128)(2,1)S(1)}, bf16[128,1024]{0,1:T(8,128)(2,1)}, u32[]{:S(2)}, u32[]{:S(2)}) collective-permute-start(bf16[128,1024]{0,1:T(8,128)(2,1)S(1)} %get-tuple-element.66), channel_id=1, source_target_pairs={{8,0},{16,8},{24,16},{32,24},{40,32},{48,40},{56,48},{64,56},{72,6... | collective-permute-start | bytes 786440 | tf_op jit(solution)/shard_map/ppermute | solution.py:15
  311.3 142.1 %copy-start.12 = (f32[128]{0:T(128)S(1)}, f32[128]{0:T(128)}, u32[]{:S(2)}) copy-start(f32[128]{0:T(128)} %iota_subtract_fusion.1) | copy-start | bytes 1540
  311.4 142.7 %copy-start.5 = (f32[2,16]{1,0:T(2,128)S(1)}, f32[2,16]{1,0:T(2,128)}, u32[]{:S(2)}) copy-start(f32[2,16]{1,0:T(2,128)} %get-tuple-element.96) | copy-start | bytes 388
  311.4 142.7 %copy-start.10 = (f32[2,16]{1,0:T(2,128)S(1)}, f32[2,16]{1,0:T(2,128)}, u32[]{:S(2)}) copy-start(f32[2,16]{1,0:T(2,128)} %get-tuple-element.103) | copy-start | bytes 388
  470.0 20.2 %all-to-all-start.1 = ((bf16[32,128,32]{1,2,0:T(8,128)(2,1)}), bf16[32,128,32]{1,2,0:T(8,128)(2,1)S(1)}, u32[]{:S(2)}, u32[]{:S(2)}) async-start(bf16[32,128,32]{1,2,0:T(8,128)(2,1)} %bitcast.27), calls=%async_computation.1 | async-start | bytes 524288 | tf_op jit(solution)/shard_map/all_to_all | solution.py:123
